TPU v7x, 512 devices: a whole 4x4x16 slice. The times are simulated.
512 devices in a mesh: dp: 128 (over x, z, core), query: 4 (over y).
Axes of the slice: x: 4, y: 4, z: 16, core: 2. Of those that a mesh axis runs over, the one named last changes fastest.
Arguments:
- train_acts: bfloat16 [512, 64, 5120], P('dp'), may hold values from -45 to 45
- train_grads: bfloat16 [512, 64, 1280], P('dp'), may hold values from -6 to 6
- timestep: int32 [512], P('dp'), may hold values from 0 to 999
- time_weight: float32 [1000], replicated, may hold values from 0.5 to 2
- query_acts: bfloat16 [512, 64, 5120], P(('dp', 'query')), may hold values from -6 to 6
- query_grads: bfloat16 [512, 64, 1280], P(('dp', 'query')), may hold values from -6 to 6
- proj_in: bfloat16 [5120, 64], replicated, may hold values from -0.078125 to 0.078125
- proj_out: bfloat16 [1280, 64], replicated, may hold values from -0.15625 to 0.15625
- damping: float32 [1], replicated, may hold values from 0.5 to 2
Outputs:
- scores: float32 [512, 512], P(('dp', 'query'))
All inputs are finite; a program needn't handle non-finite values.
Results may differ from a plain program's by a relative error of at most 0.0075.
Values may be sent and summed in bfloat16 or wider, within the bound.
A program may use at most 64 MiB of HBM per device.

v0:
```python
import jax
import jax.numpy as jnp
from jax import lax
from jax.sharding import PartitionSpec as P


def project(acts, grads, proj_in, proj_out):
    count, tok, width_in = acts.shape
    width_out = grads.shape[2]
    act_proj = jnp.dot(
        acts.reshape(count * tok, width_in), proj_in, preferred_element_type=jnp.float32
    ).astype(jnp.bfloat16)
    grad_proj = jnp.dot(
        grads.reshape(count * tok, width_out), proj_out, preferred_element_type=jnp.float32
    ).astype(jnp.bfloat16)
    act_proj = act_proj.reshape(count, tok, -1)
    grad_proj = grad_proj.reshape(count, tok, -1)
    return jnp.einsum("etr,ets->ers", grad_proj, act_proj, preferred_element_type=jnp.float32)


def inner_rows(left, right):
    return lax.dot_general(
        left, right, (((1,), (1,)), ((), ())), preferred_element_type=jnp.float32
    )


def body(
    train_acts,
    train_grads,
    timestep,
    time_weight,
    query_acts,
    query_grads,
    proj_in,
    proj_out,
    damping,
):
    count = train_acts.shape[0]
    rank = proj_in.shape[1]
    outer = project(train_acts, train_grads, proj_in, proj_out)
    onehot = (
        timestep[:, None] == jnp.arange(time_weight.shape[0], dtype=jnp.int32)[None, :]
    ).astype(jnp.float32)
    weights = jnp.sum(onehot * time_weight[None, :], axis=1)
    train_vec = (outer * weights[:, None, None]).reshape(count, rank * rank).astype(jnp.bfloat16)
    query_count = query_acts.shape[0]
    query_vec = (
        project(query_acts, query_grads, proj_in, proj_out)
        .reshape(query_count, rank * rank)
        .astype(jnp.bfloat16)
    )
    gathered = lax.all_gather(train_vec, "dp", axis=0, tiled=True)
    total = gathered.shape[0]
    kernel = inner_rows(gathered, gathered)
    trace = lax.psum(jnp.sum(train_vec.astype(jnp.float32) ** 2), "dp")
    lam = damping[0] * trace / (rank * rank)
    matrix = kernel + lam * jnp.eye(total, dtype=jnp.float32)
    cross = inner_rows(query_vec, gathered)
    factor = jnp.linalg.cholesky(matrix)
    solved = jax.scipy.linalg.cho_solve((factor, True), cross.T)
    return solved.T


def solution(mesh):
    return jax.shard_map(
        body,
        mesh=mesh,
        in_specs=(
            P("dp", None, None),
            P("dp", None, None),
            P("dp"),
            P(),
            P(("dp", "query"), None, None),
            P(("dp", "query"), None, None),
            P(),
            P(),
            P(),
        ),
        out_specs=P(("dp", "query"), None),
        check_vma=False,
    )
```

profile of v0, /device:TPU:1, one launch (start us, length us, event | category | flops | bytes accessed | tf_op | source)
XLA Modules:
  0.0 458.0 jit_solution(17711943390210514963)
XLA Ops:
  6.6 1.7 copy-done
  8.3 2.0 convolution_convert_fusion
  10.3 0.1 copy.19
  10.4 1.4 convolution_convert_fusion.1
  11.9 0.8 reshape.148
  12.6 0.2 select_reduce_fusion.4
  12.8 2.2 multiply_reduce_fusion
  15.0 1.6 reshape.176
  16.6 255.5 %psum.7 = f32[]{:T(128)} all-reduce(f32[]{:T(128)} %get-tuple-element.33), channel_id=1, replica_groups=mesh['dp'=128,'query'=4] {'dp'}, use_global_device_ids=true, to_apply=%region_2.0 | all-reduce | flops 1 | bytes 8 | tf_op jit(solution)/shard_map/psum | solution.py:55
  272.7 1.4 convolution_convert_fusion.3
  274.2 1.3 convolution_convert_fusion.2
  275.4 0.1 reshape.179
  276.3 6.9 %reshape.177 = bf16[512,4096]{1,0:T(8,128)(2,1)} reshape(bf16[128,4,4096]{2,1,0:T(4,128)(2,1)} %all-gather.3.cloned.1.call-done) | data formatting | bytes 8388608
  283.2 6.8 %fusion.63 = f32[512,512]{1,0:T(8,128)} fusion(bf16[512,4096]{1,0:T(8,128)(2,1)} %reshape.177), kind=kOutput, calls=%fused_computation.117 | convolution fusion | flops 2147483648 | bytes 5242880 | tf_op jit(solution)/shard_map/dot_general | solution.py:22
  290.0 2.6 copy.18
  292.6 1.8 fusion.14
  294.3 1.0 copy-done.2
  295.3 11.7 %cholesky.103 = f32[128,128]{1,0:T(8,128)S(1)} custom-call(f32[128,128]{1,0:T(8,128)S(1)} %cholesky.263), custom_call_target="Cholesky" | custom-call | tf_op jit(solution)/shard_map/jit(cholesky)/cholesky | solution.py:59
  307.1 9.8 %custom-call.34 = f32[1,128,128]{1,2,0:T(8,128)S(1)} custom-call(f32[1,128,128]{2,1,0:T(8,128)S(1)} %get-tuple-element.32), custom_call_target="InvertDiagBlocksLowerTriangular" | custom-call | tf_op jit(solution)/shard_map/jit(cholesky)/cholesky | solution.py:59
  316.9 1.1 cholesky.222
  318.0 1.9 constant_dynamic-update-slice_fusion.3
  320.0 1.2 convolution_subtract_fusion
  321.2 11.8 %cholesky.215 = f32[128,128]{1,0:T(8,128)S(1)} custom-call(f32[128,128]{1,0:T(8,128)S(1)} %cholesky.267), custom_call_target="Cholesky" | custom-call | tf_op jit(solution)/shard_map/jit(cholesky)/cholesky | solution.py:59
  333.1 0.7 select_reduce_fusion.2
  333.7 9.8 %custom-call.35 = f32[1,128,128]{1,2,0:T(8,128)S(1)} custom-call(f32[1,128,128]{2,1,0:T(8,128)S(1)} %get-tuple-element.29), custom_call_target="InvertDiagBlocksLowerTriangular" | custom-call | tf_op jit(solution)/shard_map/jit(cholesky)/cholesky | solution.py:59
  343.5 1.0 convolution_dynamic-update-slice_fusion
  344.5 1.4 convolution_subtract_fusion.1
  346.0 11.7 %cholesky.236 = f32[128,128]{1,0:T(8,128)S(1)} custom-call(f32[128,128]{1,0:T(8,128)S(1)} %cholesky.272), custom_call_target="Cholesky" | custom-call | tf_op jit(solution)/shard_map/jit(cholesky)/cholesky | solution.py:59
  357.7 0.6 select_reduce_fusion.1
  358.3 0.6 compare_reduce_fusion.1
  359.0 9.8 %custom-call.36 = f32[1,128,128]{1,2,0:T(8,128)S(1)} custom-call(f32[1,128,128]{2,1,0:T(8,128)S(1)} %get-tuple-element.26), custom_call_target="InvertDiagBlocksLowerTriangular" | custom-call | tf_op jit(solution)/shard_map/jit(cholesky)/cholesky | solution.py:59
  368.8 0.8 convolution_dynamic-update-slice_fusion.1
  369.6 1.4 convolution_subtract_fusion.2
  371.1 11.9 %cholesky.253 = f32[128,128]{1,0:T(8,128)S(1)} custom-call(f32[128,128]{1,0:T(8,128)S(1)} %convolution_subtract_fusion.2), custom_call_target="Cholesky" | custom-call | tf_op jit(solution)/shard_map/jit(cholesky)/cholesky | solution.py:59
  383.0 0.6 select_reduce_fusion
  383.6 0.6 compare_reduce_fusion
  384.3 0.7 compare_reduce_fusion.2
  387.5 2.3 select_select_fusion
  389.8 14.1 %while.1 = (s32[]{:T(128)}, f32[512,512]{1,0:T(8,128)}, s32[4,2]{0,1:T(2,128)S(1)}, f32[4,128,128]{2,1,0:T(8,128)}, s32[]{:T(128)}) while((s32[]{:T(128)}, f32[512,512]{1,0:T(8,128)}, s32[4,2]{0,1:T(2,128)S(1)}, f32[4,128,128]{2,1,0:T(8,128)}, s32[]{:T(128)}) %tuple.28), condition=%wide.while_cond, body=%wide.while_body.sunk | while | flops 2 | bytes 132705 | solution.py:60
  389.9 0.6 fusion.87
  390.5 2.9 bitcast_dynamic-update-slice_fusion.2
  393.5 0.6 fusion.87
  394.0 2.9 bitcast_dynamic-update-slice_fusion.2
  397.0 0.6 fusion.87
  397.6 2.9 bitcast_dynamic-update-slice_fusion.2
  400.5 0.6 fusion.87
  401.1 2.8 bitcast_dynamic-update-slice_fusion.2
  403.9 40.1 %custom-call.37 = f32[4,128,128]{1,2,0:T(8,128)S(1)} custom-call(f32[4,128,128]{2,1,0:T(8,128)} %get-tuple-element.12), custom_call_target="InvertDiagBlocksLowerTriangular" | custom-call | tf_op jit(solution)/shard_map/jit(_cho_solve)/triangular_solve | solution.py:60
  444.1 3.5 fusion.64
  447.5 0.2 fusion.36
  447.7 0.2 fusion.6
  447.9 0.2 fusion.37
  448.1 0.2 fusion.7
  448.3 0.2 fusion.38
  448.5 0.3 fusion.12
  448.8 0.2 convolution_bitcast_fusion.6
  449.0 0.2 convolution_bitcast_fusion.5
  449.2 0.2 fusion.3
  449.4 0.2 convolution_bitcast_fusion.3
  449.6 0.2 fusion.8
  449.8 0.2 convolution_bitcast_fusion.1
  450.0 0.3 fusion.10
  450.3 0.2 convolution_bitcast_fusion
  450.5 0.6 maximum_bitcast_fusion
  (26 shorter events, 0.5 us)
Async XLA Ops:
  6.5 1.8 copy-start
  6.5 266.2 %copy-start.3 = (bf16[5120,64]{0,1:T(8,128)(2,1)S(1)}, bf16[5120,64]{0,1:T(8,128)(2,1)}, u32[]{:S(2)}) copy-start(bf16[5120,64]{0,1:T(8,128)(2,1)} %param.15) | copy-start | bytes 1966084
  6.5 267.6 %copy-start.4 = (bf16[1280,64]{0,1:T(8,128)(2,1)S(1)}, bf16[1280,64]{0,1:T(8,128)(2,1)}, u32[]{:S(2)}) copy-start(bf16[1280,64]{0,1:T(8,128)(2,1)} %param.16) | copy-start | bytes 491524
  6.5 6.1 %copy-start.6 = (s32[4]{0:T(128)S(1)}, s32[4]{0:T(128)}, u32[]{:S(2)}) copy-start(s32[4]{0:T(128)} %param.11) | copy-start | bytes 52
  6.5 6.1 %copy-start.5 = (f32[1000]{0:T(1024)S(1)}, f32[1000]{0:T(1024)}, u32[]{:S(2)}) copy-start(f32[1000]{0:T(1024)} %param.12) | copy-start | bytes 12004
  6.5 269.7 %all-gather.3.cloned.1.call-start = ((), (), s32[]{:S(2)}) async-start(), calls=%async_computation | async-start | bytes 4227072 | tf_op jit(solution)/shard_map/all_gather | solution.py:52
  294.3 1.0 copy-start.2
  444.1 3.6 copy-start.1
Sparse Core Ops, SparseCore 0:
  16.7 147.6 all-gather.2
where the time goes:
time: 462 us; the launch traced here: 458 us
  blocking collectives  255 us (55%)
  other arithmetic  126 us (27%)
  local copies, waits for them, and re-layouts  30 us (6%)
  matrix products  29.3 us (6%)
  between operations  17.4 us (4%)
    psum x1, blocking collectives, body(): trace = lax.psum(jnp.sum(train_vec.astype(jnp.float32) ** 2), 'dp')  255 us
    another operation x14, other arithmetic, body(): factor = jnp.linalg.cholesky(matrix)  80.6 us
    another operation x3, other arithmetic, body(): solved = jax.scipy.linalg.cho_solve((factor, True), cross.T)  42.5 us
    another operation x12, local copies, waits for them, and re-layouts  14.1 us
    unnamed x16, local copies, waits for them, and re-layouts  11.2 us
    dot_general x2, matrix products, inner_rows(): lax.dot_general(left, right, (((1,), (1,)), ((), ())), preferred_element_...  10.3 us
  transfers between devices with their start and end apart: 1, of which 0 were waited for; matrix products, arithmetic and copies ran while one was open for 1% of the time, Pallas kernels for 0%

commit v1 on v0

v1 whole, which is shorter than its diff:
```python
import functools

import jax
import jax.numpy as jnp
from jax import lax
from jax.experimental import pallas as pl
from jax.experimental.pallas import tpu as pltpu
from jax.sharding import PartitionSpec as P

MESH = pl.DeviceIdType.MESH
BF = jnp.bfloat16
F32 = jnp.float32

NX, NZ, NC, NY = 4, 16, 2, 4
NB, NA = 4, 4
TOL = 2e-5
MAX_STEPS = 4096


def dot(a, b, dims):
    return lax.dot_general(a, b, (dims, ((), ())), preferred_element_type=F32)


def pair_tiles(m):
    return jnp.concatenate([m[:32], m[32:]], axis=1)


def gram_kernel(
    tacts_hbm, tgrads_hbm, step_ref, weight_ref, qacts_hbm, qgrads_hbm, pin_hbm, pout_hbm,
    gram_ref, cross_ref,
    tacts, tgrads, qacts, qgrads, pin, pout,
    wide, sendbuf, landing, wide2, spread, query_rows, table,
    load_sem, a_send, a_recv, b_send, b_recv, c_send, c_recv, s_send, s_recv,
):
    dp = lax.axis_index("dp")
    y = lax.axis_index("query")
    x = dp // (NZ * NC)
    z = lax.rem(dp // NC, NZ)
    c = lax.rem(dp, NC)
    a = lax.rem(z, NA)
    b = z // NA

    def device(dx=0, dz=0, dc=0, dy=0):
        x1 = lax.rem(x + (dx + NX), NX)
        z1 = lax.rem(z + (dz + NZ), NZ)
        c1 = lax.rem(c + dc, NC)
        y1 = lax.rem(y + (dy + NY), NY)
        return ((x1 * NZ + z1) * NC + c1, y1)

    loads = []
    for i, (src, dst) in enumerate(
        [(pin_hbm, pin), (pout_hbm, pout), (tacts_hbm, tacts), (tgrads_hbm, tgrads),
         (qacts_hbm, qacts), (qgrads_hbm, qgrads)]
    ):
        copy = pltpu.make_async_copy(src, dst, load_sem.at[i])
        copy.start()
        loads.append(copy)

    barrier = pltpu.get_barrier_semaphore()
    line = [
        (dj, dx, dc)
        for dj in range(NB) for dx in range(NX) for dc in range(NC)
        if (dj, dx, dc) != (0, 0, 0)
    ]
    partners = [device(dz=NA * dj, dx=dx, dc=dc) for dj, dx, dc in line]
    partners += [device(dz=d) for d in (1, -1, 2, -2)]
    partners += [device(dy=d) for d in (1, 2, 3)]
    for partner in partners:
        pl.semaphore_signal(barrier, inc=1, device_id=partner, device_id_type=MESH)

    for i in range(4):
        loads[i].wait()
    count, tok, width_in = tacts.shape
    width_out = tgrads.shape[2]
    grad_proj = dot(tgrads[...].reshape(count * tok, width_out), pout[...], ((1,), (0,))).astype(BF)
    act_proj = dot(tacts[...].reshape(count * tok, width_in), pin[...], ((1,), (0,))).astype(BF)
    for e in range(count):
        rows = slice(e * tok, (e + 1) * tok)
        outer = dot(grad_proj[rows], act_proj[rows], ((0,), (0,)))
        weight = weight_ref[step_ref[e]]
        wide[pl.ds(e, 32, stride=4), :] = pair_tiles(outer * weight)

    def tile_for(x1, c1):
        left = wide[pl.ds(pl.multiple_of(8 * (2 * x1 + c1), 8), 8), :]
        right = wide[pl.ds(pl.multiple_of(64 + 8 * (2 * y + c1), 8), 8), :]
        return jnp.concatenate([left, right], axis=0).astype(BF)

    for x1 in range(NX):
        for c1 in range(NC):
            sendbuf[2 * x1 + c1] = tile_for(x1, c1)
    me = 2 * x + c
    landing[b, me] = tile_for(x, c)

    pl.semaphore_wait(barrier, len(partners))

    sends = []
    for dj, dx, dc in line:
        x1 = lax.rem(x + dx, NX)
        c1 = lax.rem(c + dc, NC)
        copy = pltpu.make_async_remote_copy(
            src_ref=sendbuf.at[2 * x1 + c1], dst_ref=landing.at[b, me],
            send_sem=a_send.at[dj, dx, dc], recv_sem=a_recv.at[dj, dx, dc],
            device_id=device(dz=NA * dj, dx=dx, dc=dc), device_id_type=MESH,
        )
        copy.start()
        sends.append(copy)

    loads[4].wait()
    loads[5].wait()
    qg = dot(qgrads[0], pout[...], ((1,), (0,))).astype(BF)
    qa = dot(qacts[0], pin[...], ((1,), (0,))).astype(BF)
    query = pair_tiles(dot(qg, qa, ((0,), (0,))))
    for k in range(16):
        row = jnp.concatenate([query[2 * k:2 * k + 1], query[2 * k + 1:2 * k + 2]], axis=1)
        query_rows[k] = jnp.broadcast_to(row, (16, 256)).astype(BF)

    for dj, dx, dc in line:
        b1 = lax.rem(b + (NB - dj), NB)
        src = 2 * lax.rem(x + (NX - dx), NX) + lax.rem(c + dc, NC)
        pltpu.make_async_remote_copy(
            src_ref=sendbuf.at[0], dst_ref=landing.at[b1, src],
            send_sem=a_send.at[dj, dx, dc], recv_sem=a_recv.at[dj, dx, dc],
            device_id=device(dz=-NA * dj, dx=-dx, dc=dc), device_id_type=MESH,
        ).wait_recv()

    kx = 2 * x + c
    ky = 8 + 2 * y + c
    for b1 in range(NB):
        wide2[...] = landing[b1].astype(F32).reshape(128, 128)
        for t in range(4):
            for e in range(4):
                spread[t, pl.ds(e, 8, stride=4), :] = wide2[pl.ds(4 * t + e, 8, stride=16), :]
        table[kx, b1, a] = jnp.concatenate([spread[0], spread[1]], axis=1).astype(BF)
        table[ky, b1, a] = jnp.concatenate([spread[2], spread[3]], axis=1).astype(BF)

    def class_of(j):
        return lax.rem(a + (0, NA - 1, 1, 2)[j], NA)

    def move(k, j, send_sem, recv_sem, target):
        part = table.at[k, :, class_of(j)]
        return pltpu.make_async_remote_copy(
            src_ref=part, dst_ref=part, send_sem=send_sem, recv_sem=recv_sem,
            device_id=target, device_id_type=MESH,
        )

    for i, d in enumerate((1, -1, 2)):
        for kind, k in ((0, kx), (1, ky)):
            d1 = -d if (i == 2 and kind == 1) else d
            part = table.at[k, :, a]
            copy = pltpu.make_async_remote_copy(
                src_ref=part, dst_ref=part, send_sem=b_send.at[i, kind],
                recv_sem=b_recv.at[i, kind], device_id=device(dz=d1), device_id_type=MESH,
            )
            copy.start()
            sends.append(copy)

    sib = device(dc=1)

    def start(copy):
        copy.start()
        sends.append(copy)

    def fan_out(j):
        for d in (1, 3, 2):
            start(move(kx, j, c_send.at[j, 0, d], c_recv.at[j, 0, d], device(dx=d)))
            start(move(ky, j, c_send.at[j, 1, d], c_recv.at[j, 1, d], device(dy=d)))
        start(move(kx, j, s_send.at[j, 0, 0], s_recv.at[j, 0, 0], sib))
        start(move(ky, j, s_send.at[j, 1, 0], s_recv.at[j, 1, 0], sib))

    def pass_on(j):
        for d in (1, 3, 2):
            k = 2 * lax.rem(x + (NX - d), NX) + c
            move(k, j, c_send.at[j, 0, d], c_recv.at[j, 0, d], sib).wait_recv()
            start(move(k, j, s_send.at[j, 0, d], s_recv.at[j, 0, d], sib))
            k = 8 + 2 * lax.rem(y + (NY - d), NY) + c
            move(k, j, c_send.at[j, 1, d], c_recv.at[j, 1, d], sib).wait_recv()
            start(move(k, j, s_send.at[j, 1, d], s_recv.at[j, 1, d], sib))

    fan_out(0)
    for j in (1, 2, 3):
        for kind, k in ((0, kx), (1, ky)):
            move(k, j, b_send.at[j - 1, kind], b_recv.at[j - 1, kind], sib).wait_recv()
        fan_out(j)
    for j in range(4):
        pass_on(j)
    for j in range(4):
        for d in range(4):
            k = 2 * lax.rem(x + (NX - d), NX) + (1 - c)
            move(k, j, s_send.at[j, 0, d], s_recv.at[j, 0, d], sib).wait_recv()
            k = 8 + 2 * lax.rem(y + (NY - d), NY) + (1 - c)
            move(k, j, s_send.at[j, 1, d], s_recv.at[j, 1, d], sib).wait_recv()

    gram_ref[...] = jnp.zeros_like(gram_ref)
    cross_ref[...] = jnp.zeros_like(cross_ref)

    def accumulate(i, carry):
        rows = jnp.concatenate(
            [table[4 * i + k].reshape(512, 256) for k in range(4)], axis=1
        )
        queries = jnp.concatenate([query_rows[4 * i + k] for k in range(4)], axis=1)
        product = dot(jnp.concatenate([rows, queries], axis=0), rows, ((1,), (1,)))
        gram_ref[...] += product[:512]
        cross_ref[...] += product[512:520]
        return carry

    lax.fori_loop(0, 4, accumulate, 0)

    for copy in sends:
        copy.wait_send()


def solve_kernel(gram_ref, cross_ref, damping_ref, out_ref, column):
    rank2 = 4096.0
    eye = (
        lax.broadcasted_iota(jnp.int32, (128, 128), 0)
        == lax.broadcasted_iota(jnp.int32, (128, 128), 1)
    )
    diagonal = jnp.concatenate(
        [
            jnp.sum(
                jnp.where(eye, gram_ref[128 * t:128 * t + 128, 128 * t:128 * t + 128], 0.0),
                axis=0, keepdims=True,
            )
            for t in range(4)
        ],
        axis=1,
    )

    def total(v):
        return jnp.sum(v, axis=1, keepdims=True)

    lam = damping_ref[0] * total(diagonal) / rank2
    top = jnp.max(diagonal, axis=1, keepdims=True) + lam
    scale = 1.0 / top
    lam_scaled = lam * scale
    jacobi = 1.0 / (diagonal * scale + lam_scaled)
    size = jnp.max(jnp.abs(cross_ref[0:1]), axis=1, keepdims=True)
    size = jnp.where(size > 0.0, size, 1.0)
    bound = (TOL * lam_scaled) * (TOL * lam_scaled)

    def product(p):
        parts = [jnp.zeros((8, 128), F32) for _ in range(4)]
        for t in range(4):
            chunk = p[:, 128 * t:128 * t + 128]
            spread = jnp.broadcast_to(chunk, (128, 128)).T
            for u in range(4):
                tile = gram_ref[128 * t:128 * t + 128, 128 * u:128 * u + 128] * spread
                parts[u] += jnp.sum(tile.reshape(16, 8, 128), axis=0)
        whole = jnp.concatenate([jnp.sum(v, axis=0, keepdims=True) for v in parts], axis=1)
        return whole * scale + lam_scaled * p

    def go_on(state):
        step, more = state[0], state[1]
        return jnp.logical_and(step < MAX_STEPS, more)

    def advance(state):
        step, _, s, r, p, rz = state
        q = product(p)
        alpha = rz / total(p * q)
        s = s + alpha * p
        r = r - alpha * q
        u = r * jacobi
        rz_new = total(r * u)
        p = u + (rz_new / rz) * p
        more = (total(r * r) - bound * total(s * s))[0, 0] > 0.0
        return step + 1, more, s, r, p, rz_new

    r = cross_ref[0:1] / size
    u = r * jacobi
    rz = total(r * u)
    more = rz[0, 0] > 0.0
    state = (jnp.int32(0), more, jnp.zeros_like(r), r, u, rz)
    s = lax.while_loop(go_on, advance, state)[2] * (size * scale)

    for t in range(4):
        column[128 * t:128 * t + 128, :] = jnp.broadcast_to(s[:, 128 * t:128 * t + 128], (128, 128)).T
    for x in range(NX):
        rows = jnp.concatenate(
            [column[32 * z + 8 * x:32 * z + 8 * x + 8, :] for z in range(NZ)], axis=0
        )
        out_ref[:, 128 * x:128 * x + 128] = rows.T[0:1, :]


def body(
    train_acts, train_grads, timestep, time_weight, query_acts, query_grads, proj_in, proj_out,
    damping,
):
    any_spec = pl.BlockSpec(memory_space=pl.ANY)
    smem = pl.BlockSpec(memory_space=pltpu.SMEM)
    vmem = pl.BlockSpec(memory_space=pltpu.VMEM)
    dma = pltpu.SemaphoreType.DMA
    gram, cross = pl.pallas_call(
        gram_kernel,
        out_shape=(
            jax.ShapeDtypeStruct((512, 512), F32),
            jax.ShapeDtypeStruct((8, 512), F32),
        ),
        in_specs=[any_spec, any_spec, smem, smem, any_spec, any_spec, any_spec, any_spec],
        out_specs=(vmem, vmem),
        scratch_shapes=[
            pltpu.VMEM(train_acts.shape, BF),
            pltpu.VMEM(train_grads.shape, BF),
            pltpu.VMEM(query_acts.shape, BF),
            pltpu.VMEM(query_grads.shape, BF),
            pltpu.VMEM(proj_in.shape, BF),
            pltpu.VMEM(proj_out.shape, BF),
            pltpu.VMEM((128, 128), F32),
            pltpu.VMEM((8, 16, 128), BF),
            pltpu.VMEM((NB, 8, 16, 128), BF),
            pltpu.VMEM((128, 128), F32),
            pltpu.VMEM((4, 32, 128), F32),
            pltpu.VMEM((16, 16, 256), BF),
            pltpu.VMEM((16, NB, NA, 32, 256), BF),
            dma((6,)),
            dma((NB, NX, NC)),
            dma((NB, NX, NC)),
            dma((3, 2)),
            dma((3, 2)),
            dma((4, 2, 4)),
            dma((4, 2, 4)),
            dma((4, 2, 4)),
            dma((4, 2, 4)),
        ],
        compiler_params=pltpu.CompilerParams(
            collective_id=0, has_side_effects=True, vmem_limit_bytes=40 << 20
        ),
        name="gather_gram",
    )(train_acts, train_grads, timestep, time_weight, query_acts, query_grads, proj_in, proj_out)
    return pl.pallas_call(
        solve_kernel,
        out_shape=jax.ShapeDtypeStruct((1, 512), F32),
        in_specs=[vmem, vmem, smem],
        out_specs=vmem,
        scratch_shapes=[pltpu.VMEM((512, 128), F32)],
        compiler_params=pltpu.CompilerParams(vmem_limit_bytes=16 << 20),
        name="solve",
    )(gram, cross, damping)


def solution(mesh):
    return jax.shard_map(
        body,
        mesh=mesh,
        in_specs=(
            P("dp", None, None),
            P("dp", None, None),
            P("dp"),
            P(),
            P(("dp", "query"), None, None),
            P(("dp", "query"), None, None),
            P(),
            P(),
            P(),
        ),
        out_specs=P(("dp", "query"), None),
        check_vma=False,
    )
```

time: 462 us -> 66.4 us (0.14)
  blocking collectives: 255 us -> 0 us
  other arithmetic: 126 us -> 0 us
  Pallas kernels: 0 us -> 58.6 us
  matrix products: 29.3 us -> 0 us
  local copies, waits for them, and re-layouts: 30 us -> 6.89 us
  between operations: 17.4 us -> 0.7 us
    psum x1 -> x0, blocking collectives: 255 us -> none  [body(): trace = lax.psum(jnp.sum(train_vec.astype(jnp.float32) ** 2), 'dp')]
    another operation x17 -> x0, other arithmetic: 123 us -> none  [the longest x14 80.6 us: body(): factor = jnp.linalg.cholesky(matrix)]
    pallas_call x0 -> x2, Pallas kernels: none -> 58.6 us  [the longest x1 53.5 us: body(): pl.pallas_call(gram_kernel, out_shape=(jax.ShapeDtypeStruct((512, 512), F...]
    dot_general x7 -> x0, matrix products: 18.6 us -> none  [the longest x2 10.3 us: inner_rows(): lax.dot_general(left, right, (((1,), (1,)), ((), ())), preferred_element_...]
    another operation x17 -> x0, local copies, waits for them, and re-layouts: 15.3 us -> none
    another operation x20 -> x0, matrix products: 10.8 us -> none  [the longest x6 7.86 us: body(): factor = jnp.linalg.cholesky(matrix)]
    unnamed x16 -> x14, local copies, waits for them, and re-layouts: 11.2 us -> 6.89 us
  transfers between devices with their start and end apart: 1 -> 0, of which waited for: 0 -> 0; matrix products, arithmetic and copies ran while one was open for 1% -> 0% of each run, Pallas kernels for 0% -> 0%
where the time goes in v1:
time: 66.4 us; the launch traced here: 66.1 us
  Pallas kernels  58.6 us (88%)
  local copies, waits for them, and re-layouts  6.89 us (10%)
  between operations  0.7 us (1%)
    pallas_call x1, Pallas kernels, body(): pl.pallas_call(gram_kernel, out_shape=(jax.ShapeDtypeStruct((512, 512), F...  53.5 us
    unnamed x14, local copies, waits for them, and re-layouts  6.89 us
    pallas_call x1, Pallas kernels, body(): pl.pallas_call(solve_kernel, out_shape=jax.ShapeDtypeStruct((1, 512), F32...  5.06 us

profile of v1, /device:TPU:1, one launch (start us, length us, event | category | flops | bytes accessed | tf_op | source)
XLA Modules:
  0.0 66.1 jit_solution(1901496260362492496)
XLA Ops:
  0.0 0.0 copy-start.1
  0.0 0.0 copy-start.2
  0.0 1.8 %copy.10.pin_hbm = bf16[5120,64]{1,0:T(8,128)(2,1)S(1)} copy(bf16[5120,64]{0,1:T(8,128)(2,1)} %param.15) | data formatting | bytes 1310720 | tf_op args[6]
  1.8 1.1 %copy.11.pout_hbm = bf16[1280,64]{1,0:T(8,128)(2,1)S(1)} copy(bf16[1280,64]{0,1:T(8,128)(2,1)} %param.16) | data formatting | bytes 327680 | tf_op args[7]
  2.9 0.0 copy-done.1
  2.9 0.0 copy-done.2
  2.9 0.0 copy-start
  2.9 1.7 %copy-done = bf16[4,64,5120]{2,1,0:T(8,128)(2,1)S(1)} copy-done((bf16[4,64,5120]{2,1,0:T(8,128)(2,1)S(1)}, bf16[4,64,5120]{2,1,0:T(8,128)(2,1)}, u32[]{:S(2)}) %copy-start) | copy-done | bytes 2621464
  4.7 0.0 copy-start.3
  4.7 0.9 %copy-done.3 = bf16[1,64,1280]{2,1,0:T(8,128)(2,1)S(1)} copy-done((bf16[1,64,1280]{2,1,0:T(8,128)(2,1)S(1)}, bf16[1,64,1280]{2,1,0:T(8,128)(2,1)}, u32[]{:S(2)}) %copy-start.3) | copy-done | bytes 163864
  5.6 0.0 copy-start.4
  5.6 0.7 %copy-done.4 = f32[1000]{0:T(1024)S(1)} copy-done((f32[1000]{0:T(1024)S(1)}, f32[1000]{0:T(1024)}, u32[]{:S(2)}) %copy-start.4) | copy-done | bytes 4024
  6.3 0.0 copy-start.5
  6.3 0.7 copy-done.5
  6.9 53.5 %gather_gram.1 = (f32[512,512]{1,0:T(8,128)S(1)}, f32[8,512]{1,0:T(8,128)S(1)}) custom-call(bf16[4,64,5120]{2,1,0:T(8,128)(2,1)S(1)} %copy-done, bf16[4,64,1280]{2,1,0:T(8,128)(2,1)S(1)} %copy-done.1, s32[4]{0:T(128)S(1)} %copy-done.5, f32[1000]{0:T(1024)S(1)} %copy-done.4, bf16[1,64,5120]{2,1,0:T(8,128)(2,1)S(1)} %copy-done.2, ...), custom_call_target="tpu_custom_call" | custom-call | tf_op jit(solution)/shard_map/gather_gram/pallas_call | solution.py:292
  61.1 5.1 %solve.1 = f32[1,512]{1,0:T(1,128)} custom-call(f32[512,512]{1,0:T(8,128)S(1)} %get-tuple-element.7.gram_ref, f32[8,512]{1,0:T(8,128)S(1)} %get-tuple-element.8.cross_ref, f32[1]{0:T(128)S(6)} %copy.12.damping_ref), custom_call_target="tpu_custom_call" | custom-call | tf_op jit(solution)/shard_map/solve/pallas_call | solution.py:329
Async XLA Ops:
  0.0 2.9 %copy-start.1 = (bf16[4,64,1280]{2,1,0:T(8,128)(2,1)S(1)}, bf16[4,64,1280]{2,1,0:T(8,128)(2,1)}, u32[]{:S(2)}) copy-start(bf16[4,64,1280]{2,1,0:T(8,128)(2,1)} %tgrads_hbm.1) | copy-start | bytes 1966084
  0.0 2.9 %copy-start.2 = (bf16[1,64,5120]{2,1,0:T(8,128)(2,1)S(1)}, bf16[1,64,5120]{2,1,0:T(8,128)(2,1)}, u32[]{:S(2)}) copy-start(bf16[1,64,5120]{2,1,0:T(8,128)(2,1)} %qacts_hbm.1) | copy-start | bytes 1966084
  2.9 1.7 %copy-start = (bf16[4,64,5120]{2,1,0:T(8,128)(2,1)S(1)}, bf16[4,64,5120]{2,1,0:T(8,128)(2,1)}, u32[]{:S(2)}) copy-start(bf16[4,64,5120]{2,1,0:T(8,128)(2,1)} %tacts_hbm.1) | copy-start | bytes 7864324
  4.7 0.9 %copy-start.3 = (bf16[1,64,1280]{2,1,0:T(8,128)(2,1)S(1)}, bf16[1,64,1280]{2,1,0:T(8,128)(2,1)}, u32[]{:S(2)}) copy-start(bf16[1,64,1280]{2,1,0:T(8,128)(2,1)} %qgrads_hbm.1) | copy-start | bytes 491524
  5.6 0.7 %copy-start.4 = (f32[1000]{0:T(1024)S(1)}, f32[1000]{0:T(1024)}, u32[]{:S(2)}) copy-start(f32[1000]{0:T(1024)} %weight_ref.1) | copy-start | bytes 12004
  6.3 0.7 copy-start.5

commit v2 on v1

v2 whole, which is shorter than its diff:
```python
import functools

import jax
import jax.numpy as jnp
from jax import lax
from jax.experimental import pallas as pl
from jax.experimental.pallas import tpu as pltpu
from jax.sharding import PartitionSpec as P

MESH = pl.DeviceIdType.MESH
BF = jnp.bfloat16
F32 = jnp.float32

NX, NZ, NC, NY = 4, 16, 2, 4
FAR = (0, 5, -5)
NEAR = {1: (1, 0), -1: (-1, 0), 2: (2, 0), -2: (-2, 0), 6: (1, 5), 4: (-1, 5), -6: (-1, -5),
        -4: (1, -5), 7: (2, 5), 3: (-2, 5), -7: (-2, -5), -3: (2, -5)}
LAST = ((3, 5), (-3, -5))
LAG = 13
TOL = 2e-5
MAX_STEPS = 4096


def dot(a, b, dims):
    return lax.dot_general(a, b, (dims, ((), ())), preferred_element_type=F32)


def pair_tiles(m):
    return jnp.concatenate([m[:32], m[32:]], axis=1)


def gram_kernel(
    tacts_hbm, tgrads_hbm, step_hbm, weight_hbm, qacts_hbm, qgrads_hbm, pin_hbm, pout_hbm,
    gram_ref, cross_ref,
    tacts, tgrads, qacts, qgrads, pin, pout, step_ref, weight_ref,
    wide, sendbuf, landing, wide2, spread, query_rows, table,
    load_sem, a_send, a_recv, b_send, b_recv, c_send, c_recv, s_send, s_recv,
):
    dp = lax.axis_index("dp")
    y = lax.axis_index("query")
    x = dp // (NZ * NC)
    z = lax.rem(dp // NC, NZ)
    c = lax.rem(dp, NC)

    def device(dx=0, dz=0, dc=0, dy=0):
        x1 = lax.rem(x + (dx + NX), NX)
        z1 = lax.rem(z + (dz + NZ), NZ)
        c1 = lax.rem(c + dc, NC)
        y1 = lax.rem(y + (dy + NY), NY)
        return ((x1 * NZ + z1) * NC + c1, y1)

    loads = []
    for i, (src, dst) in enumerate(
        [(step_hbm, step_ref), (weight_hbm, weight_ref), (pout_hbm, pout), (tgrads_hbm, tgrads),
         (pin_hbm, pin), (tacts_hbm, tacts), (qgrads_hbm, qgrads), (qacts_hbm, qacts)]
    ):
        copy = pltpu.make_async_copy(src, dst, load_sem.at[i])
        copy.start()
        loads.append(copy)

    barrier = pltpu.get_barrier_semaphore()
    line = [
        (i, dx, dc)
        for i in range(len(FAR)) for dx in range(NX) for dc in range(NC)
        if (i, dx, dc) != (0, 0, 0)
    ]
    partners = [device(dz=FAR[i], dx=dx, dc=dc) for i, dx, dc in line]
    partners += [device(dz=d) for d in (1, -1, 2, -2, 3, -3)]
    partners += [device(dy=d) for d in (1, 2, 3)]
    for partner in partners:
        pl.semaphore_signal(barrier, inc=1, device_id=partner, device_id_type=MESH)

    for i in range(6):
        loads[i].wait()
    count, tok, width_in = tacts.shape
    width_out = tgrads.shape[2]
    grad_proj = dot(tgrads[...].reshape(count * tok, width_out), pout[...], ((1,), (1,))).astype(BF)
    act_proj = dot(tacts[...].reshape(count * tok, width_in), pin[...], ((1,), (1,))).astype(BF)
    for e in range(count):
        rows = slice(e * tok, (e + 1) * tok)
        outer = dot(grad_proj[rows], act_proj[rows], ((0,), (0,)))
        weight = weight_ref[step_ref[e]]
        wide[pl.ds(e, 32, stride=4), :] = pair_tiles(outer * weight)

    def tile_for(x1, c1):
        left = wide[pl.ds(pl.multiple_of(8 * (2 * x1 + c1), 8), 8), :]
        right = wide[pl.ds(pl.multiple_of(64 + 8 * (2 * y + c1), 8), 8), :]
        return jnp.concatenate([left, right], axis=0).astype(BF)

    for x1 in range(NX):
        for c1 in range(NC):
            sendbuf[2 * x1 + c1] = tile_for(x1, c1)
    me = 2 * x + c
    landing[me] = tile_for(x, c)

    pl.semaphore_wait(barrier, len(partners))

    for i, dx, dc in line:
        x1 = lax.rem(x + dx, NX)
        c1 = lax.rem(c + dc, NC)
        pltpu.make_async_remote_copy(
            src_ref=sendbuf.at[2 * x1 + c1], dst_ref=landing.at[8 * i + me],
            send_sem=a_send, recv_sem=a_recv.at[i, dx, dc],
            device_id=device(dz=-FAR[i], dx=dx, dc=dc), device_id_type=MESH,
        ).start()

    loads[6].wait()
    loads[7].wait()
    qg = dot(qgrads[0], pout[...], ((1,), (1,))).astype(BF)
    qa = dot(qacts[0], pin[...], ((1,), (1,))).astype(BF)
    query = pair_tiles(dot(qg, qa, ((0,), (0,))))
    for k in range(16):
        row = jnp.concatenate([query[2 * k:2 * k + 1], query[2 * k + 1:2 * k + 2]], axis=1)
        query_rows[k] = jnp.broadcast_to(row, (16, 256)).astype(BF)

    kx = 2 * x + c
    ky = 8 + 2 * y + c
    sib = device(dc=1)

    def plane(o):
        return lax.rem(z + (o + NZ), NZ)

    def take(i):
        for i1, dx, dc in line:
            if i1 == i:
                src = 2 * lax.rem(x + (NX - dx), NX) + lax.rem(c + dc, NC)
                pltpu.make_async_remote_copy(
                    src_ref=sendbuf.at[0], dst_ref=landing.at[8 * i + src],
                    send_sem=a_send, recv_sem=a_recv.at[i, dx, dc],
                    device_id=sib, device_id_type=MESH,
                ).wait_recv()
        wide2[...] = landing[8 * i:8 * i + 8].astype(F32).reshape(128, 128)
        for t in range(4):
            for e in range(4):
                spread[t, pl.ds(e, 8, stride=4), :] = wide2[pl.ds(4 * t + e, 8, stride=16), :]
        o = plane(FAR[i])
        table[kx, o] = jnp.concatenate([spread[0], spread[1]], axis=1).astype(BF)
        table[ky, o] = jnp.concatenate([spread[2], spread[3]], axis=1).astype(BF)

    def move(k, o, send_sem, recv_sem, target):
        part = table.at[k, plane(o)]
        return pltpu.make_async_remote_copy(
            src_ref=part, dst_ref=part, send_sem=send_sem, recv_sem=recv_sem,
            device_id=target, device_id_type=MESH,
        )

    def relay(s):
        for o, (n, s1) in NEAR.items():
            if s1 == s:
                move(kx, s, b_send, b_recv.at[o + 7, 0], device(dz=-n)).start()
                move(ky, s, b_send, b_recv.at[o + 7, 1], device(dz=-n)).start()
        for kind, k in ((0, kx), (1, ky)):
            if LAST[kind][1] == s:
                move(k, s, b_send, b_recv.at[15, kind], device(dz=-LAST[kind][0])).start()

    def relayed(o):
        move(kx, o, b_send, b_recv.at[o + 7, 0], sib).wait_recv()
        move(ky, o, b_send, b_recv.at[o + 7, 1], sib).wait_recv()

    def fan_out(o):
        for d in (1, 3, 2):
            move(kx, o, c_send, c_recv.at[o + 7, 0, d], device(dx=d)).start()
            move(ky, o, c_send, c_recv.at[o + 7, 1, d], device(dy=d)).start()
        move(kx, o, s_send, s_recv, sib).start()
        move(ky, o, s_send, s_recv, sib).start()

    def pass_on(o):
        for d in (1, 3, 2):
            k = 2 * lax.rem(x + (NX - d), NX) + c
            move(k, o, c_send, c_recv.at[o + 7, 0, d], sib).wait_recv()
            move(k, o, s_send, s_recv, sib).start()
            k = 8 + 2 * lax.rem(y + (NY - d), NY) + c
            move(k, o, c_send, c_recv.at[o + 7, 1, d], sib).wait_recv()
            move(k, o, s_send, s_recv, sib).start()

    for i, s in enumerate(FAR):
        take(i)
        relay(s)
        fan_out(s)
    order = (*FAR, *NEAR, 8)
    passed = 0
    for done, o in enumerate((*NEAR, 8), len(FAR) + 1):
        relayed(o)
        fan_out(o)
        while passed < done - LAG:
            pass_on(order[passed])
            passed += 1
    for o in order[passed:]:
        pass_on(o)

    def drain(part, sem):
        pltpu.make_async_copy(part, part, sem).wait()

    drain(table.at[0:8], s_recv)

    gram_ref[...] = jnp.zeros_like(gram_ref)
    cross_ref[...] = jnp.zeros_like(cross_ref)

    def accumulate(i, carry):
        rows = jnp.concatenate(
            [table[4 * i + k].reshape(512, 256) for k in range(4)], axis=1
        )
        queries = jnp.concatenate([query_rows[4 * i + k] for k in range(4)], axis=1)
        product = dot(jnp.concatenate([rows, queries], axis=0), rows, ((1,), (1,)))
        gram_ref[...] += product[:512]
        cross_ref[...] += product[512:520]
        return carry

    lax.fori_loop(0, 4, accumulate, 0)

    drain(landing.at[0:len(line)], a_send)
    drain(table.at[0:2, 0:len(NEAR) + 1], b_send)
    drain(table.at[0:6], c_send)
    drain(table.at[0:8], s_send)


def solve_kernel(gram_ref, cross_ref, damping_ref, out_ref, column):
    rank2 = 4096.0
    eye = (
        lax.broadcasted_iota(jnp.int32, (128, 128), 0)
        == lax.broadcasted_iota(jnp.int32, (128, 128), 1)
    )
    diagonal = jnp.concatenate(
        [
            jnp.sum(
                jnp.where(eye, gram_ref[128 * t:128 * t + 128, 128 * t:128 * t + 128], 0.0),
                axis=0, keepdims=True,
            )
            for t in range(4)
        ],
        axis=1,
    )

    def total(v):
        return jnp.sum(v, axis=1, keepdims=True)

    lam = damping_ref[0] * total(diagonal) / rank2
    top = jnp.max(diagonal, axis=1, keepdims=True) + lam
    scale = 1.0 / top
    lam_scaled = lam * scale
    jacobi = 1.0 / (diagonal * scale + lam_scaled)
    size = jnp.max(jnp.abs(cross_ref[0:1]), axis=1, keepdims=True)
    size = jnp.where(size > 0.0, size, 1.0)
    bound = (TOL * lam_scaled) * (TOL * lam_scaled)

    def product(p):
        parts = [jnp.zeros((8, 128), F32) for _ in range(4)]
        for t in range(4):
            chunk = p[:, 128 * t:128 * t + 128]
            spread = jnp.broadcast_to(chunk, (128, 128)).T
            for u in range(4):
                tile = gram_ref[128 * t:128 * t + 128, 128 * u:128 * u + 128] * spread
                parts[u] += jnp.sum(tile.reshape(16, 8, 128), axis=0)
        whole = jnp.concatenate([jnp.sum(v, axis=0, keepdims=True) for v in parts], axis=1)
        return whole * scale + lam_scaled * p

    def go_on(state):
        step, more = state[0], state[1]
        return jnp.logical_and(step < MAX_STEPS, more)

    def advance(state):
        step, _, s, r, p, rz = state
        q = product(p)
        alpha = rz / total(p * q)
        s = s + alpha * p
        r = r - alpha * q
        u = r * jacobi
        rz_new = total(r * u)
        p = u + (rz_new / rz) * p
        more = (total(r * r) - bound * total(s * s))[0, 0] > 0.0
        return step + 1, more, s, r, p, rz_new

    r = cross_ref[0:1] / size
    u = r * jacobi
    rz = total(r * u)
    more = rz[0, 0] > 0.0
    state = (jnp.int32(0), more, jnp.zeros_like(r), r, u, rz)
    s = lax.while_loop(go_on, advance, state)[2] * (size * scale)

    for t in range(4):
        column[128 * t:128 * t + 128, :] = jnp.broadcast_to(s[:, 128 * t:128 * t + 128], (128, 128)).T
    for x in range(NX):
        rows = jnp.concatenate(
            [column[32 * z + 8 * x:32 * z + 8 * x + 8, :] for z in range(NZ)], axis=0
        )
        out_ref[:, 128 * x:128 * x + 128] = rows.T[0:1, :]


def body(
    train_acts, train_grads, timestep, time_weight, query_acts, query_grads, proj_in, proj_out,
    damping,
):
    any_spec = pl.BlockSpec(memory_space=pl.ANY)
    smem = pl.BlockSpec(memory_space=pltpu.SMEM)
    vmem = pl.BlockSpec(memory_space=pltpu.VMEM)
    dma = pltpu.SemaphoreType.DMA
    gram, cross = pl.pallas_call(
        gram_kernel,
        out_shape=(
            jax.ShapeDtypeStruct((512, 512), F32),
            jax.ShapeDtypeStruct((8, 512), F32),
        ),
        in_specs=[any_spec] * 8,
        out_specs=(vmem, vmem),
        scratch_shapes=[
            pltpu.VMEM(train_acts.shape, BF),
            pltpu.VMEM(train_grads.shape, BF),
            pltpu.VMEM(query_acts.shape, BF),
            pltpu.VMEM(query_grads.shape, BF),
            pltpu.VMEM(proj_in.shape[::-1], BF),
            pltpu.VMEM(proj_out.shape[::-1], BF),
            pltpu.SMEM(timestep.shape, jnp.int32),
            pltpu.SMEM(time_weight.shape, F32),
            pltpu.VMEM((128, 128), F32),
            pltpu.VMEM((8, 16, 128), BF),
            pltpu.VMEM((8 * len(FAR), 16, 128), BF),
            pltpu.VMEM((128, 128), F32),
            pltpu.VMEM((4, 32, 128), F32),
            pltpu.VMEM((16, 16, 256), BF),
            pltpu.VMEM((16, NZ, 32, 256), BF),
            dma((8,)),
            dma,
            dma((len(FAR), NX, NC)),
            dma,
            dma((NZ, 2)),
            dma,
            dma((NZ, 2, 4)),
            dma,
            dma,
        ],
        compiler_params=pltpu.CompilerParams(
            collective_id=0, has_side_effects=True, vmem_limit_bytes=62 << 20
        ),
        name="gather_gram",
    )(train_acts, train_grads, timestep, time_weight, query_acts, query_grads, proj_in.T, proj_out.T)
    return pl.pallas_call(
        solve_kernel,
        out_shape=jax.ShapeDtypeStruct((1, 512), F32),
        in_specs=[vmem, vmem, smem],
        out_specs=vmem,
        scratch_shapes=[pltpu.VMEM((512, 128), F32)],
        compiler_params=pltpu.CompilerParams(vmem_limit_bytes=16 << 20),
        name="solve",
    )(gram, cross, damping)


def solution(mesh):
    return jax.shard_map(
        body,
        mesh=mesh,
        in_specs=(
            P("dp", None, None),
            P("dp", None, None),
            P("dp"),
            P(),
            P(("dp", "query"), None, None),
            P(("dp", "query"), None, None),
            P(),
            P(),
            P(),
        ),
        out_specs=P(("dp", "query"), None),
        check_vma=False,
    )
```

time: 66.4 us -> 53.8 us (0.81)
  Pallas kernels: 58.6 us -> 51 us
  local copies, waits for them, and re-layouts: 6.89 us -> 1.93 us
    pallas_call x1, Pallas kernels: 53.5 us -> 45.9 us  [body(): pl.pallas_call(gram_kernel, out_shape=(jax.ShapeDtypeStruct((512, 512), F...]
    unnamed x14 -> x4, local copies, waits for them, and re-layouts: 6.89 us -> 1.93 us
where the time goes in v2:
time: 53.8 us; the launch traced here: 53.6 us
  Pallas kernels  51 us (95%)
  local copies, waits for them, and re-layouts  1.93 us (4%)
  between operations  0.67 us (1%)
    pallas_call x1, Pallas kernels, body(): pl.pallas_call(gram_kernel, out_shape=(jax.ShapeDtypeStruct((512, 512), F...  45.9 us
    pallas_call x1, Pallas kernels, body(): pl.pallas_call(solve_kernel, out_shape=jax.ShapeDtypeStruct((1, 512), F32...  5.06 us
    unnamed x4, local copies, waits for them, and re-layouts  1.93 us

profile of v2, /device:TPU:1, one launch (start us, length us, event | category | flops | bytes accessed | tf_op | source)
XLA Modules:
  0.0 53.6 jit_solution(11529810157872425185)
XLA Ops:
  0.7 45.9 %gather_gram.1 = (f32[512,512]{1,0:T(8,128)}, f32[8,512]{1,0:T(8,128)}) custom-call(bf16[4,64,5120]{2,1,0:T(8,128)(2,1)} %tacts_hbm.1, bf16[4,64,1280]{2,1,0:T(8,128)(2,1)} %tgrads_hbm.1, s32[4]{0:T(128)} %step_hbm.1, f32[1000]{0:T(1024)} %weight_hbm.1, bf16[1,64,5120]{2,1,0:T(8,128)(2,1)} %qacts_hbm.1, bf16[1,64,1280]{2,1,0:T(8,128)(2,1)} %qgrads_hbm.1, ...), custom_call_target="tpu_custom_call" | custom-call | tf_op jit(solution)/shard_map/gather_gram/pallas_call | solution.py:297
  46.6 0.0 copy-start
  46.6 1.2 %copy-done = f32[512,512]{1,0:T(8,128)S(1)} copy-done((f32[512,512]{1,0:T(8,128)S(1)}, f32[512,512]{1,0:T(8,128)}, u32[]{:S(2)}) %copy-start) | copy-done | bytes 1048600
  47.8 0.0 copy-start.1
  47.8 0.7 %copy-done.1 = f32[8,512]{1,0:T(8,128)S(1)} copy-done((f32[8,512]{1,0:T(8,128)S(1)}, f32[8,512]{1,0:T(8,128)}, u32[]{:S(2)}) %copy-start.1) | copy-done | bytes 16408
  48.5 5.1 %solve.1 = f32[1,512]{1,0:T(1,128)} custom-call(f32[512,512]{1,0:T(8,128)S(1)} %copy-done, f32[8,512]{1,0:T(8,128)S(1)} %copy-done.1, f32[1]{0:T(128)S(6)} %copy.10.damping_ref), custom_call_target="tpu_custom_call" | custom-call | tf_op jit(solution)/shard_map/solve/pallas_call | solution.py:336
Async XLA Ops:
  46.6 1.2 %copy-start = (f32[512,512]{1,0:T(8,128)S(1)}, f32[512,512]{1,0:T(8,128)}, u32[]{:S(2)}) copy-start(f32[512,512]{1,0:T(8,128)} %get-tuple-element.7.gram_ref) | copy-start | bytes 3145732
  47.8 0.7 %copy-start.1 = (f32[8,512]{1,0:T(8,128)S(1)}, f32[8,512]{1,0:T(8,128)}, u32[]{:S(2)}) copy-start(f32[8,512]{1,0:T(8,128)} %get-tuple-element.8.cross_ref) | copy-start | bytes 49156

commit v3 on v2

--- a/solution.py
+++ b/solution.py
@@ -16,8 +16,10 @@
 NEAR = {1: (1, 0), -1: (-1, 0), 2: (2, 0), -2: (-2, 0), 6: (1, 5), 4: (-1, 5), -6: (-1, -5),
         -4: (1, -5), 7: (2, 5), 3: (-2, 5), -7: (-2, -5), -3: (2, -5)}
 LAST = ((3, 5), (-3, -5))
-LAG = 13
-TOL = 2e-5
+ORDER = (*FAR, *NEAR, 8)
+HALF = len(ORDER) // 2
+SCHEDULE = (0, 5, -5, 1, -1, 2, -2, 6, 4, -6, -4, 7, 3, -7, -3, 8)
+TOL = 1e-4
 MAX_STEPS = 4096
 
 
@@ -33,7 +35,7 @@
     tacts_hbm, tgrads_hbm, step_hbm, weight_hbm, qacts_hbm, qgrads_hbm, pin_hbm, pout_hbm,
     gram_ref, cross_ref,
     tacts, tgrads, qacts, qgrads, pin, pout, step_ref, weight_ref,
-    wide, sendbuf, landing, wide2, spread, query_rows, table,
+    wide, sendbuf, landing, wide2, spread, query_rows, table, lower_ref,
     load_sem, a_send, a_recv, b_send, b_recv, c_send, c_recv, s_send, s_recv,
 ):
     dp = lax.axis_index("dp")
@@ -116,9 +118,6 @@
     kx = 2 * x + c
     ky = 8 + 2 * y + c
     sib = device(dc=1)
-
-    def plane(o):
-        return lax.rem(z + (o + NZ), NZ)
 
     def take(i):
         for i1, dx, dc in line:
@@ -133,80 +132,95 @@
         for t in range(4):
             for e in range(4):
                 spread[t, pl.ds(e, 8, stride=4), :] = wide2[pl.ds(4 * t + e, 8, stride=16), :]
-        o = plane(FAR[i])
+        o = ORDER.index(FAR[i])
         table[kx, o] = jnp.concatenate([spread[0], spread[1]], axis=1).astype(BF)
         table[ky, o] = jnp.concatenate([spread[2], spread[3]], axis=1).astype(BF)
 
-    def move(k, o, send_sem, recv_sem, target):
-        part = table.at[k, plane(o)]
+    def move(k, o, send_sem, recv_sem, target, to=None):
+        slot = ORDER.index(o)
         return pltpu.make_async_remote_copy(
-            src_ref=part, dst_ref=part, send_sem=send_sem, recv_sem=recv_sem,
-            device_id=target, device_id_type=MESH,
+            src_ref=table.at[k, slot],
+            dst_ref=table.at[k, slot if to is None else ORDER.index(to)],
+            send_sem=send_sem, recv_sem=recv_sem, device_id=target, device_id_type=MESH,
         )
 
     def relay(s):
         for o, (n, s1) in NEAR.items():
             if s1 == s:
-                move(kx, s, b_send, b_recv.at[o + 7, 0], device(dz=-n)).start()
-                move(ky, s, b_send, b_recv.at[o + 7, 1], device(dz=-n)).start()
+                move(kx, s, b_send, b_recv.at[o + 7, 0], device(dz=-n), o).start()
+                move(ky, s, b_send, b_recv.at[o + 7, 1], device(dz=-n), o).start()
         for kind, k in ((0, kx), (1, ky)):
             if LAST[kind][1] == s:
-                move(k, s, b_send, b_recv.at[15, kind], device(dz=-LAST[kind][0])).start()
+                move(k, s, b_send, b_recv.at[15, kind], device(dz=-LAST[kind][0]), 8).start()
 
     def relayed(o):
         move(kx, o, b_send, b_recv.at[o + 7, 0], sib).wait_recv()
         move(ky, o, b_send, b_recv.at[o + 7, 1], sib).wait_recv()
+
+    def to_sib(k, o):
+        half = ORDER.index(o) // HALF
+        move(k, o, s_send, s_recv.at[half], sib).start()
 
     def fan_out(o):
         for d in (1, 3, 2):
             move(kx, o, c_send, c_recv.at[o + 7, 0, d], device(dx=d)).start()
             move(ky, o, c_send, c_recv.at[o + 7, 1, d], device(dy=d)).start()
-        move(kx, o, s_send, s_recv, sib).start()
-        move(ky, o, s_send, s_recv, sib).start()
+        to_sib(kx, o)
+        to_sib(ky, o)
 
     def pass_on(o):
         for d in (1, 3, 2):
             k = 2 * lax.rem(x + (NX - d), NX) + c
             move(k, o, c_send, c_recv.at[o + 7, 0, d], sib).wait_recv()
-            move(k, o, s_send, s_recv, sib).start()
+            to_sib(k, o)
             k = 8 + 2 * lax.rem(y + (NY - d), NY) + c
             move(k, o, c_send, c_recv.at[o + 7, 1, d], sib).wait_recv()
-            move(k, o, s_send, s_recv, sib).start()
-
-    for i, s in enumerate(FAR):
-        take(i)
-        relay(s)
-        fan_out(s)
-    order = (*FAR, *NEAR, 8)
-    passed = 0
-    for done, o in enumerate((*NEAR, 8), len(FAR) + 1):
-        relayed(o)
-        fan_out(o)
-        while passed < done - LAG:
-            pass_on(order[passed])
-            passed += 1
-    for o in order[passed:]:
-        pass_on(o)
+            to_sib(k, o)
+
+    for step in SCHEDULE:
+        if step in FAR:
+            take(FAR.index(step))
+            relay(step)
+        else:
+            relayed(step)
+        fan_out(step)
 
     def drain(part, sem):
         pltpu.make_async_copy(part, part, sem).wait()
 
-    drain(table.at[0:8], s_recv)
-
-    gram_ref[...] = jnp.zeros_like(gram_ref)
-    cross_ref[...] = jnp.zeros_like(cross_ref)
-
-    def accumulate(i, carry):
-        rows = jnp.concatenate(
-            [table[4 * i + k].reshape(512, 256) for k in range(4)], axis=1
-        )
+    for o in ORDER[:HALF]:
+        pass_on(o)
+    drain(table.at[0:4], s_recv.at[0])
+
+    def rows(k, lower):
+        part = table[k, HALF:] if lower else table[k, :HALF]
+        return part.reshape(256, 256)
+
+    def first(i, total):
+        upper = jnp.concatenate([rows(4 * i + k, False) for k in range(4)], axis=1)
+        return total + dot(upper, upper, ((1,), (1,)))
+
+    gram_ref[:256, :256] = lax.fori_loop(0, 4, first, jnp.zeros((256, 256), F32))
+
+    for o in ORDER[HALF:]:
+        pass_on(o)
+    drain(table.at[0:4], s_recv.at[1])
+
+    lower_ref[...] = jnp.zeros_like(lower_ref)
+
+    def second(i, carry):
+        upper = jnp.concatenate([rows(4 * i + k, False) for k in range(4)], axis=1)
+        lower = jnp.concatenate([rows(4 * i + k, True) for k in range(4)], axis=1)
         queries = jnp.concatenate([query_rows[4 * i + k] for k in range(4)], axis=1)
-        product = dot(jnp.concatenate([rows, queries], axis=0), rows, ((1,), (1,)))
-        gram_ref[...] += product[:512]
-        cross_ref[...] += product[512:520]
+        left = jnp.concatenate([lower, queries], axis=0)
+        lower_ref[:, :256] += dot(left, upper, ((1,), (1,)))
+        lower_ref[:, 256:] += dot(left, lower, ((1,), (1,)))
         return carry
 
-    lax.fori_loop(0, 4, accumulate, 0)
+    lax.fori_loop(0, 4, second, 0)
+    gram_ref[256:] = lower_ref[:256]
+    gram_ref[:256, 256:] = lower_ref[:256, :256].T
+    cross_ref[...] = lower_ref[256:264]
 
     drain(landing.at[0:len(line)], a_send)
     drain(table.at[0:2, 0:len(NEAR) + 1], b_send)
@@ -214,7 +228,7 @@
     drain(table.at[0:8], s_send)
 
 
-def solve_kernel(gram_ref, cross_ref, damping_ref, out_ref, column):
+def solve_kernel(gram_ref, cross_ref, damping_ref, out_ref, column, ordered):
     rank2 = 4096.0
     eye = (
         lax.broadcasted_iota(jnp.int32, (128, 128), 0)
@@ -259,38 +273,43 @@
         return jnp.logical_and(step < MAX_STEPS, more)
 
     def advance(state):
-        step, _, s, r, p, rz = state
-        q = product(p)
-        alpha = rz / total(p * q)
-        s = s + alpha * p
-        r = r - alpha * q
+        step, _, s, r, p, v, old_rz, old_alpha = state
+        more = (total(r * r) - bound * total(s * s))[0, 0] > 0.0
         u = r * jacobi
-        rz_new = total(r * u)
-        p = u + (rz_new / rz) * p
-        more = (total(r * r) - bound * total(s * s))[0, 0] > 0.0
-        return step + 1, more, s, r, p, rz_new
+        rz = total(r * u)
+        beta = rz / old_rz
+        w = product(u)
+        curve = total(w * u) - beta * rz / old_alpha
+        good = curve > 0.0
+        alpha = jnp.where(good, rz / curve, 0.0)
+        p = u + beta * p
+        v = w + beta * v
+        old_rz = jnp.where(good, rz, jnp.inf)
+        old_alpha = jnp.where(good, alpha, 1.0)
+        return step + 1, more, s + alpha * p, r - alpha * v, p, v, old_rz, old_alpha
 
     r = cross_ref[0:1] / size
-    u = r * jacobi
-    rz = total(r * u)
-    more = rz[0, 0] > 0.0
-    state = (jnp.int32(0), more, jnp.zeros_like(r), r, u, rz)
+    zero = jnp.zeros_like(r)
+    one = jnp.ones((1, 1), F32)
+    state = (jnp.int32(0), jnp.bool_(True), zero, r, zero, zero, jnp.inf * one, one)
     s = lax.while_loop(go_on, advance, state)[2] * (size * scale)
 
+    z = lax.rem(lax.axis_index("dp") // NC, NZ)
     for t in range(4):
         column[128 * t:128 * t + 128, :] = jnp.broadcast_to(s[:, 128 * t:128 * t + 128], (128, 128)).T
+    for slot, o in enumerate(ORDER):
+        at = pl.multiple_of(8 * lax.rem(z + (o + NZ), NZ), 8)
+        for x in range(NX):
+            ordered[pl.ds(128 * x + at, 8), :] = column[32 * slot + 8 * x:32 * slot + 8 * x + 8, :]
     for x in range(NX):
-        rows = jnp.concatenate(
-            [column[32 * z + 8 * x:32 * z + 8 * x + 8, :] for z in range(NZ)], axis=0
-        )
-        out_ref[:, 128 * x:128 * x + 128] = rows.T[0:1, :]
+        out_ref[:, 128 * x:128 * x + 128] = ordered[128 * x:128 * x + 128, :].T[0:1, :]
 
 
 def body(
     train_acts, train_grads, timestep, time_weight, query_acts, query_grads, proj_in, proj_out,
     damping,
 ):
-    any_spec = pl.BlockSpec(memory_space=pl.ANY)
+    hbm = pl.BlockSpec(memory_space=pltpu.HBM)
     smem = pl.BlockSpec(memory_space=pltpu.SMEM)
     vmem = pl.BlockSpec(memory_space=pltpu.VMEM)
     dma = pltpu.SemaphoreType.DMA
@@ -300,7 +319,7 @@
             jax.ShapeDtypeStruct((512, 512), F32),
             jax.ShapeDtypeStruct((8, 512), F32),
         ),
-        in_specs=[any_spec] * 8,
+        in_specs=[hbm] * 8,
         out_specs=(vmem, vmem),
         scratch_shapes=[
             pltpu.VMEM(train_acts.shape, BF),
@@ -318,6 +337,7 @@
             pltpu.VMEM((4, 32, 128), F32),
             pltpu.VMEM((16, 16, 256), BF),
             pltpu.VMEM((16, NZ, 32, 256), BF),
+            pltpu.VMEM((272, 512), F32),
             dma((8,)),
             dma,
             dma((len(FAR), NX, NC)),
@@ -326,19 +346,27 @@
             dma,
             dma((NZ, 2, 4)),
             dma,
-            dma,
+            dma((2,)),
         ],
         compiler_params=pltpu.CompilerParams(
-            collective_id=0, has_side_effects=True, vmem_limit_bytes=62 << 20
+            collective_id=0, has_side_effects=True, vmem_limit_bytes=40 << 20
         ),
         name="gather_gram",
-    )(train_acts, train_grads, timestep, time_weight, query_acts, query_grads, proj_in.T, proj_out.T)
+    )(
+        *[
+            pltpu.with_memory_space_constraint(operand, pltpu.HBM)
+            for operand in (
+                train_acts, train_grads, timestep, time_weight, query_acts, query_grads,
+                proj_in.T, proj_out.T,
+            )
+        ]
+    )
     return pl.pallas_call(
         solve_kernel,
         out_shape=jax.ShapeDtypeStruct((1, 512), F32),
         in_specs=[vmem, vmem, smem],
         out_specs=vmem,
-        scratch_shapes=[pltpu.VMEM((512, 128), F32)],
+        scratch_shapes=[pltpu.VMEM((512, 128), F32)] * 2,
         compiler_params=pltpu.CompilerParams(vmem_limit_bytes=16 << 20),
         name="solve",
     )(gram, cross, damping)

time: 53.8 us -> 49.5 us (0.920)
  Pallas kernels: 51 us -> 48.7 us
  local copies, waits for them, and re-layouts: 1.93 us -> 0 us
    pallas_call x1, Pallas kernels: 45.9 us -> 44 us  [body(): pl.pallas_call(gram_kernel, out_shape=(jax.ShapeDtypeStruct((512, 512), F...]
    unnamed x4 -> x0, local copies, waits for them, and re-layouts: 1.93 us -> none
where the time goes in v3:
time: 49.5 us; the launch traced here: 49.3 us
  Pallas kernels  48.7 us (98%)
  between operations  0.66 us (1%)
    pallas_call x1, Pallas kernels, body(): pl.pallas_call(gram_kernel, out_shape=(jax.ShapeDtypeStruct((512, 512), F...  44 us
    pallas_call x1, Pallas kernels, body(): pl.pallas_call(solve_kernel, out_shape=jax.ShapeDtypeStruct((1, 512), F32...  4.72 us

profile of v3, /device:TPU:1, one launch (start us, length us, event | category | flops | bytes accessed | tf_op | source)
XLA Modules:
  0.0 49.3 jit_solution(9967102004866250930)
XLA Ops:
  0.7 44.0 %gather_gram.1 = (f32[512,512]{1,0:T(8,128)S(1)}, f32[8,512]{1,0:T(8,128)S(1)}) custom-call(bf16[4,64,5120]{2,1,0:T(8,128)(2,1)} %tacts_hbm.1, bf16[4,64,1280]{2,1,0:T(8,128)(2,1)} %tgrads_hbm.1, s32[4]{0:T(128)} %step_hbm.1, f32[1000]{0:T(1024)} %weight_hbm.1, bf16[1,64,5120]{2,1,0:T(8,128)(2,1)} %qacts_hbm.1, bf16[1,64,1280]{2,1,0:T(8,128)(2,1)} %qgrads_hbm.1, ...), custom_call_target="tpu_custom_call" | custom-call | tf_op jit(solution)/shard_map/gather_gram/pallas_call | solution.py:316
  44.6 4.7 %solve.1 = f32[1,512]{1,0:T(1,128)} custom-call(f32[512,512]{1,0:T(8,128)S(1)} %get-tuple-element.7.gram_ref, f32[8,512]{1,0:T(8,128)S(1)} %get-tuple-element.8.cross_ref, f32[1]{0:T(128)S(6)} %copy.10.damping_ref), custom_call_target="tpu_custom_call" | custom-call | tf_op jit(solution)/shard_map/solve/pallas_call | solution.py:364

commit v4 on v3

--- a/solution.py
+++ b/solution.py
@@ -13,12 +13,11 @@
 
 NX, NZ, NC, NY = 4, 16, 2, 4
 FAR = (0, 5, -5)
-NEAR = {1: (1, 0), -1: (-1, 0), 2: (2, 0), -2: (-2, 0), 6: (1, 5), 4: (-1, 5), -6: (-1, -5),
-        -4: (1, -5), 7: (2, 5), 3: (-2, 5), -7: (-2, -5), -3: (2, -5)}
-LAST = ((3, 5), (-3, -5))
+NEAR = {1: (1, 0), -1: (-1, 0), 2: (2, 0), -2: (-2, 0), 6: (1, 5), 4: (-1, 5), -6: (-1, -5), -4: (1, -5), 3: (1, 2), -3: (-1, -2), 7: (1, 6), -7: (-1, -6)}
+LAST = ((2, 6), (-2, -6))
 ORDER = (*FAR, *NEAR, 8)
 HALF = len(ORDER) // 2
-SCHEDULE = (0, 5, -5, 1, -1, 2, -2, 6, 4, -6, -4, 7, 3, -7, -3, 8)
+SCHEDULE = (0, 1, -1, 5, -5, 2, -2, 6, -6, 4, -4, 3, -3, 7, -7, 8)
 TOL = 1e-4
 MAX_STEPS = 4096
 
@@ -35,8 +34,9 @@
     tacts_hbm, tgrads_hbm, step_hbm, weight_hbm, qacts_hbm, qgrads_hbm, pin_hbm, pout_hbm,
     gram_ref, cross_ref,
     tacts, tgrads, qacts, qgrads, pin, pout, step_ref, weight_ref,
-    wide, sendbuf, landing, wide2, spread, query_rows, table, lower_ref,
-    load_sem, a_send, a_recv, b_send, b_recv, c_send, c_recv, s_send, s_recv,
+    wide, sendbuf, landing, wide2, spread, query_rows, sib_query, both, table,
+    part0, part1, part2, inbox0, inbox1, inbox2,
+    load_sem, a_send, a_recv, b_send, b_recv, c_send, c_recv, q_send, q_recv, s_send, s_recv,
 ):
     dp = lax.axis_index("dp")
     y = lax.axis_index("query")
@@ -72,12 +72,16 @@
     for partner in partners:
         pl.semaphore_signal(barrier, inc=1, device_id=partner, device_id_type=MESH)
 
-    for i in range(6):
-        loads[i].wait()
     count, tok, width_in = tacts.shape
     width_out = tgrads.shape[2]
+    loads[2].wait()
+    loads[3].wait()
     grad_proj = dot(tgrads[...].reshape(count * tok, width_out), pout[...], ((1,), (1,))).astype(BF)
+    loads[4].wait()
+    loads[5].wait()
     act_proj = dot(tacts[...].reshape(count * tok, width_in), pin[...], ((1,), (1,))).astype(BF)
+    loads[0].wait()
+    loads[1].wait()
     for e in range(count):
         rows = slice(e * tok, (e + 1) * tok)
         outer = dot(grad_proj[rows], act_proj[rows], ((0,), (0,)))
@@ -102,7 +106,7 @@
         c1 = lax.rem(c + dc, NC)
         pltpu.make_async_remote_copy(
             src_ref=sendbuf.at[2 * x1 + c1], dst_ref=landing.at[8 * i + me],
-            send_sem=a_send, recv_sem=a_recv.at[i, dx, dc],
+            send_sem=a_send, recv_sem=a_recv.at[i],
             device_id=device(dz=-FAR[i], dx=dx, dc=dc), device_id_type=MESH,
         ).start()
 
@@ -113,21 +117,22 @@
     query = pair_tiles(dot(qg, qa, ((0,), (0,))))
     for k in range(16):
         row = jnp.concatenate([query[2 * k:2 * k + 1], query[2 * k + 1:2 * k + 2]], axis=1)
-        query_rows[k] = jnp.broadcast_to(row, (16, 256)).astype(BF)
-
-    kx = 2 * x + c
-    ky = 8 + 2 * y + c
+        query_rows[k % 2, k // 2] = jnp.broadcast_to(row, (16, 256)).astype(BF)
     sib = device(dc=1)
+    query_copy = pltpu.make_async_remote_copy(
+        src_ref=query_rows.at[1 - c], dst_ref=sib_query, send_sem=q_send, recv_sem=q_recv,
+        device_id=sib, device_id_type=MESH,
+    )
+    query_copy.start()
+
+    kx = x
+    ky = NX + y
+
+    def drain(part, sem):
+        pltpu.make_async_copy(part, part, sem).wait()
 
     def take(i):
-        for i1, dx, dc in line:
-            if i1 == i:
-                src = 2 * lax.rem(x + (NX - dx), NX) + lax.rem(c + dc, NC)
-                pltpu.make_async_remote_copy(
-                    src_ref=sendbuf.at[0], dst_ref=landing.at[8 * i + src],
-                    send_sem=a_send, recv_sem=a_recv.at[i, dx, dc],
-                    device_id=sib, device_id_type=MESH,
-                ).wait_recv()
+        drain(landing.at[0:sum(i1 == i for i1, _, _ in line)], a_recv.at[i])
         wide2[...] = landing[8 * i:8 * i + 8].astype(F32).reshape(128, 128)
         for t in range(4):
             for e in range(4):
@@ -147,85 +152,85 @@
     def relay(s):
         for o, (n, s1) in NEAR.items():
             if s1 == s:
-                move(kx, s, b_send, b_recv.at[o + 7, 0], device(dz=-n), o).start()
-                move(ky, s, b_send, b_recv.at[o + 7, 1], device(dz=-n), o).start()
+                move(kx, s, b_send, b_recv.at[ORDER.index(o)], device(dz=-n), o).start()
+                move(ky, s, b_send, b_recv.at[ORDER.index(o)], device(dz=-n), o).start()
         for kind, k in ((0, kx), (1, ky)):
             if LAST[kind][1] == s:
-                move(k, s, b_send, b_recv.at[15, kind], device(dz=-LAST[kind][0]), 8).start()
+                move(k, s, b_send, b_recv.at[ORDER.index(8)], device(dz=-LAST[kind][0]), 8).start()
 
     def relayed(o):
-        move(kx, o, b_send, b_recv.at[o + 7, 0], sib).wait_recv()
-        move(ky, o, b_send, b_recv.at[o + 7, 1], sib).wait_recv()
-
-    def to_sib(k, o):
-        half = ORDER.index(o) // HALF
-        move(k, o, s_send, s_recv.at[half], sib).start()
+        drain(table.at[0, 0:2], b_recv.at[ORDER.index(o)])
 
     def fan_out(o):
         for d in (1, 3, 2):
-            move(kx, o, c_send, c_recv.at[o + 7, 0, d], device(dx=d)).start()
-            move(ky, o, c_send, c_recv.at[o + 7, 1, d], device(dy=d)).start()
-        to_sib(kx, o)
-        to_sib(ky, o)
-
-    def pass_on(o):
-        for d in (1, 3, 2):
-            k = 2 * lax.rem(x + (NX - d), NX) + c
-            move(k, o, c_send, c_recv.at[o + 7, 0, d], sib).wait_recv()
-            to_sib(k, o)
-            k = 8 + 2 * lax.rem(y + (NY - d), NY) + c
-            move(k, o, c_send, c_recv.at[o + 7, 1, d], sib).wait_recv()
-            to_sib(k, o)
+            move(kx, o, c_send, c_recv.at[ORDER.index(o)], device(dx=d)).start()
+            move(ky, o, c_send, c_recv.at[ORDER.index(o)], device(dy=d)).start()
+
+    def spread_out(o):
+        drain(table.at[0, 0:6], c_recv.at[ORDER.index(o)])
 
     for step in SCHEDULE:
         if step in FAR:
             take(FAR.index(step))
-            relay(step)
         else:
             relayed(step)
+        relay(step)
         fan_out(step)
 
-    def drain(part, sem):
-        pltpu.make_async_copy(part, part, sem).wait()
+    def exchange(i, mine, theirs):
+        copy = pltpu.make_async_remote_copy(
+            src_ref=mine, dst_ref=theirs, send_sem=s_send.at[i], recv_sem=s_recv.at[i],
+            device_id=sib, device_id_type=MESH,
+        )
+        copy.start()
+        return copy
+
+    def rows(i, lower):
+        parts = [table[4 * i + k, HALF:] if lower else table[4 * i + k, :HALF] for k in range(4)]
+        return jnp.concatenate([part.reshape(256, 256) for part in parts], axis=1)
 
     for o in ORDER[:HALF]:
-        pass_on(o)
-    drain(table.at[0:4], s_recv.at[0])
-
-    def rows(k, lower):
-        part = table[k, HALF:] if lower else table[k, :HALF]
-        return part.reshape(256, 256)
-
-    def first(i, total):
-        upper = jnp.concatenate([rows(4 * i + k, False) for k in range(4)], axis=1)
-        return total + dot(upper, upper, ((1,), (1,)))
-
-    gram_ref[:256, :256] = lax.fori_loop(0, 4, first, jnp.zeros((256, 256), F32))
+        spread_out(o)
+    query_copy.wait()
+    own_row = lax.broadcasted_iota(jnp.int32, (16, 256), 0) < 8
+    for k in range(8):
+        both[k] = jnp.where(
+            own_row, query_rows[c, k].astype(F32), sib_query[k].astype(F32)
+        ).astype(BF)
+
+    def queries(i):
+        return jnp.concatenate([both[4 * i + k] for k in range(4)], axis=1)
+
+    upper = [rows(i, False) for i in range(2)]
+    part0[...] = dot(upper[0], upper[0], ((1,), (1,))) + dot(upper[1], upper[1], ((1,), (1,)))
+    copies = [exchange(0, part0, inbox0)]
 
     for o in ORDER[HALF:]:
-        pass_on(o)
-    drain(table.at[0:4], s_recv.at[1])
-
-    lower_ref[...] = jnp.zeros_like(lower_ref)
-
-    def second(i, carry):
-        upper = jnp.concatenate([rows(4 * i + k, False) for k in range(4)], axis=1)
-        lower = jnp.concatenate([rows(4 * i + k, True) for k in range(4)], axis=1)
-        queries = jnp.concatenate([query_rows[4 * i + k] for k in range(4)], axis=1)
-        left = jnp.concatenate([lower, queries], axis=0)
-        lower_ref[:, :256] += dot(left, upper, ((1,), (1,)))
-        lower_ref[:, 256:] += dot(left, lower, ((1,), (1,)))
-        return carry
-
-    lax.fori_loop(0, 4, second, 0)
-    gram_ref[256:] = lower_ref[:256]
-    gram_ref[:256, 256:] = lower_ref[:256, :256].T
-    cross_ref[...] = lower_ref[256:264]
+        spread_out(o)
+    left = [jnp.concatenate([rows(i, True), queries(i)], axis=0) for i in range(2)]
+    upper = [rows(i, False) for i in range(2)]
+    part1[...] = dot(left[0], upper[0], ((1,), (1,))) + dot(left[1], upper[1], ((1,), (1,)))
+    copies.append(exchange(1, part1, inbox1))
+    left = [jnp.concatenate([rows(i, True), queries(i)], axis=0) for i in range(2)]
+    part2[...] = dot(left[0], left[0][:256], ((1,), (1,))) + dot(left[1], left[1][:256], ((1,), (1,)))
+    copies.append(exchange(2, part2, inbox2))
+
+    copies[0].wait_recv()
+    gram_ref[:256, :256] = part0[...] + inbox0[...]
+    copies[1].wait_recv()
+    corner = part1[:256] + inbox1[:256]
+    gram_ref[256:, :256] = corner
+    gram_ref[:256, 256:] = corner.T
+    cross_ref[:, :256] = part1[256:264] + inbox1[264:272]
+    copies[2].wait_recv()
+    gram_ref[256:, 256:] = part2[:256] + inbox2[:256]
+    cross_ref[:, 256:] = part2[256:264] + inbox2[264:272]
 
     drain(landing.at[0:len(line)], a_send)
     drain(table.at[0:2, 0:len(NEAR) + 1], b_send)
     drain(table.at[0:6], c_send)
-    drain(table.at[0:8], s_send)
+    for copy in copies:
+        copy.wait_send()
 
 
 def solve_kernel(gram_ref, cross_ref, damping_ref, out_ref, column, ordered):
@@ -335,18 +340,27 @@
             pltpu.VMEM((8 * len(FAR), 16, 128), BF),
             pltpu.VMEM((128, 128), F32),
             pltpu.VMEM((4, 32, 128), F32),
-            pltpu.VMEM((16, 16, 256), BF),
-            pltpu.VMEM((16, NZ, 32, 256), BF),
-            pltpu.VMEM((272, 512), F32),
+            pltpu.VMEM((2, 8, 16, 256), BF),
+            pltpu.VMEM((8, 16, 256), BF),
+            pltpu.VMEM((8, 16, 256), BF),
+            pltpu.VMEM((8, NZ, 32, 256), BF),
+            pltpu.VMEM((256, 256), F32),
+            pltpu.VMEM((272, 256), F32),
+            pltpu.VMEM((272, 256), F32),
+            pltpu.VMEM((256, 256), F32),
+            pltpu.VMEM((272, 256), F32),
+            pltpu.VMEM((272, 256), F32),
             dma((8,)),
             dma,
-            dma((len(FAR), NX, NC)),
+            dma((len(FAR),)),
             dma,
-            dma((NZ, 2)),
+            dma((NZ,)),
             dma,
-            dma((NZ, 2, 4)),
+            dma((NZ,)),
             dma,
-            dma((2,)),
+            dma,
+            dma((3,)),
+            dma((3,)),
         ],
         compiler_params=pltpu.CompilerParams(
             collective_id=0, has_side_effects=True, vmem_limit_bytes=40 << 20

time: 49.5 us -> 45.9 us (0.927)
  Pallas kernels: 48.7 us -> 45.1 us
    pallas_call x1, Pallas kernels: 44 us -> 41.4 us  [body(): pl.pallas_call(gram_kernel, out_shape=(jax.ShapeDtypeStruct((512, 512), F...]
    pallas_call x1, Pallas kernels: 4.72 us -> 3.72 us  [body(): pl.pallas_call(solve_kernel, out_shape=jax.ShapeDtypeStruct((1, 512), F32...]
where the time goes in v4:
time: 45.9 us; the launch traced here: 45.8 us
  Pallas kernels  45.1 us (98%)
  between operations  0.66 us (1%)
    pallas_call x1, Pallas kernels, body(): pl.pallas_call(gram_kernel, out_shape=(jax.ShapeDtypeStruct((512, 512), F...  41.4 us
    pallas_call x1, Pallas kernels, body(): pl.pallas_call(solve_kernel, out_shape=jax.ShapeDtypeStruct((1, 512), F32...  3.72 us

profile of v4, /device:TPU:1, one launch (start us, length us, event | category | flops | bytes accessed | tf_op | source)
XLA Modules:
  0.0 45.8 jit_solution(3841397109021717165)
XLA Ops:
  0.7 41.4 %gather_gram.1 = (f32[512,512]{1,0:T(8,128)S(1)}, f32[8,512]{1,0:T(8,128)S(1)}) custom-call(bf16[4,64,5120]{2,1,0:T(8,128)(2,1)} %tacts_hbm.1, bf16[4,64,1280]{2,1,0:T(8,128)(2,1)} %tgrads_hbm.1, s32[4]{0:T(128)} %step_hbm.1, f32[1000]{0:T(1024)} %weight_hbm.1, bf16[1,64,5120]{2,1,0:T(8,128)(2,1)} %qacts_hbm.1, bf16[1,64,1280]{2,1,0:T(8,128)(2,1)} %qgrads_hbm.1, ...), custom_call_target="tpu_custom_call" | custom-call | tf_op jit(solution)/shard_map/gather_gram/pallas_call | solution.py:321
  42.0 3.7 %solve.1 = f32[1,512]{1,0:T(1,128)} custom-call(f32[512,512]{1,0:T(8,128)S(1)} %get-tuple-element.7.gram_ref, f32[8,512]{1,0:T(8,128)S(1)} %get-tuple-element.8.cross_ref, f32[1]{0:T(128)S(6)} %copy.10.damping_ref), custom_call_target="tpu_custom_call" | custom-call | tf_op jit(solution)/shard_map/solve/pallas_call | solution.py:378

commit v5 on v4

--- a/solution.py
+++ b/solution.py
@@ -67,7 +67,7 @@
         if (i, dx, dc) != (0, 0, 0)
     ]
     partners = [device(dz=FAR[i], dx=dx, dc=dc) for i, dx, dc in line]
-    partners += [device(dz=d) for d in (1, -1, 2, -2, 3, -3)]
+    partners += [device(dz=d) for d in (1, -1, 2, -2)]
     partners += [device(dy=d) for d in (1, 2, 3)]
     for partner in partners:
         pl.semaphore_signal(barrier, inc=1, device_id=partner, device_id_type=MESH)
@@ -152,22 +152,19 @@
     def relay(s):
         for o, (n, s1) in NEAR.items():
             if s1 == s:
-                move(kx, s, b_send, b_recv.at[ORDER.index(o)], device(dz=-n), o).start()
-                move(ky, s, b_send, b_recv.at[ORDER.index(o)], device(dz=-n), o).start()
+                move(kx, s, b_send, b_recv.at[ORDER.index(o) - len(FAR)], device(dz=-n), o).start()
+                move(ky, s, b_send, b_recv.at[ORDER.index(o) - len(FAR)], device(dz=-n), o).start()
         for kind, k in ((0, kx), (1, ky)):
             if LAST[kind][1] == s:
-                move(k, s, b_send, b_recv.at[ORDER.index(8)], device(dz=-LAST[kind][0]), 8).start()
+                move(k, s, b_send, b_recv.at[ORDER.index(8) - len(FAR)], device(dz=-LAST[kind][0]), 8).start()
 
     def relayed(o):
-        drain(table.at[0, 0:2], b_recv.at[ORDER.index(o)])
+        drain(table.at[0, 0:2], b_recv.at[ORDER.index(o) - len(FAR)])
 
     def fan_out(o):
         for d in (1, 3, 2):
-            move(kx, o, c_send, c_recv.at[ORDER.index(o)], device(dx=d)).start()
-            move(ky, o, c_send, c_recv.at[ORDER.index(o)], device(dy=d)).start()
-
-    def spread_out(o):
-        drain(table.at[0, 0:6], c_recv.at[ORDER.index(o)])
+            move(kx, o, c_send, c_recv.at[ORDER.index(o) // HALF], device(dx=d)).start()
+            move(ky, o, c_send, c_recv.at[ORDER.index(o) // HALF], device(dy=d)).start()
 
     for step in SCHEDULE:
         if step in FAR:
@@ -189,8 +186,7 @@
         parts = [table[4 * i + k, HALF:] if lower else table[4 * i + k, :HALF] for k in range(4)]
         return jnp.concatenate([part.reshape(256, 256) for part in parts], axis=1)
 
-    for o in ORDER[:HALF]:
-        spread_out(o)
+    drain(table.at[0:3], c_recv.at[0])
     query_copy.wait()
     own_row = lax.broadcasted_iota(jnp.int32, (16, 256), 0) < 8
     for k in range(8):
@@ -205,8 +201,7 @@
     part0[...] = dot(upper[0], upper[0], ((1,), (1,))) + dot(upper[1], upper[1], ((1,), (1,)))
     copies = [exchange(0, part0, inbox0)]
 
-    for o in ORDER[HALF:]:
-        spread_out(o)
+    drain(table.at[0:3], c_recv.at[1])
     left = [jnp.concatenate([rows(i, True), queries(i)], axis=0) for i in range(2)]
     upper = [rows(i, False) for i in range(2)]
     part1[...] = dot(left[0], upper[0], ((1,), (1,))) + dot(left[1], upper[1], ((1,), (1,)))
@@ -354,9 +349,9 @@
             dma,
             dma((len(FAR),)),
             dma,
-            dma((NZ,)),
+            dma((len(ORDER) - len(FAR),)),
             dma,
-            dma((NZ,)),
+            dma((2,)),
             dma,
             dma,
             dma((3,)),

time: 45.9 us -> 46.2 us (level)
    pallas_call x1, Pallas kernels: 3.72 us -> 4.22 us  [body(): pl.pallas_call(solve_kernel, out_shape=jax.ShapeDtypeStruct((1, 512), F32...]
where the time goes in v5:
time: 46.2 us; the launch traced here: 46.1 us
  Pallas kernels  45.5 us (98%)
  between operations  0.66 us (1%)
    pallas_call x1, Pallas kernels, body(): pl.pallas_call(gram_kernel, out_shape=(jax.ShapeDtypeStruct((512, 512), F...  41.2 us
    pallas_call x1, Pallas kernels, body(): pl.pallas_call(solve_kernel, out_shape=jax.ShapeDtypeStruct((1, 512), F32...  4.22 us

profile of v5, /device:TPU:1, one launch (start us, length us, event | category | flops | bytes accessed | tf_op | source)
XLA Modules:
  0.0 46.1 jit_solution(4636076408150936562)
XLA Ops:
  0.7 41.2 %gather_gram.1 = (f32[512,512]{1,0:T(8,128)S(1)}, f32[8,512]{1,0:T(8,128)S(1)}) custom-call(bf16[4,64,5120]{2,1,0:T(8,128)(2,1)} %tacts_hbm.1, bf16[4,64,1280]{2,1,0:T(8,128)(2,1)} %tgrads_hbm.1, s32[4]{0:T(128)} %step_hbm.1, f32[1000]{0:T(1024)} %weight_hbm.1, bf16[1,64,5120]{2,1,0:T(8,128)(2,1)} %qacts_hbm.1, bf16[1,64,1280]{2,1,0:T(8,128)(2,1)} %qgrads_hbm.1, ...), custom_call_target="tpu_custom_call" | custom-call | tf_op jit(solution)/shard_map/gather_gram/pallas_call | solution.py:316
  41.9 4.2 %solve.1 = f32[1,512]{1,0:T(1,128)} custom-call(f32[512,512]{1,0:T(8,128)S(1)} %get-tuple-element.7.gram_ref, f32[8,512]{1,0:T(8,128)S(1)} %get-tuple-element.8.cross_ref, f32[1]{0:T(128)S(6)} %copy.10.damping_ref), custom_call_target="tpu_custom_call" | custom-call | tf_op jit(solution)/shard_map/solve/pallas_call | solution.py:373
